TPU v7x, 128 devices: a whole 4x4x4 slice. The times are simulated.
128 devices in a mesh: space: 16 (over z, y_lo, core), tracer: 8 (over x, y_hi).
Axes of the slice: x: 4, y: 4 (y_hi: 2, y_lo: 2; y = y_hi * 2 + y_lo), z: 4, core: 2. Of those that a mesh axis runs over, the one named last changes fastest.
Arguments:
- mixing_ratio_field: float32 [256, 2, 256, 256], P('tracer', None, 'space'), may hold values from 0.1 to 10
- eastward_face_cfl: float32 [2, 256, 256], P(None, 'space'), may hold values from 0.05 to 0.45
- northward_face_cfl: float32 [2, 256, 256], P(None, 'space'), may hold values from 0.05 to 0.45
- upward_face_cfl: float32 [2, 256, 256], P(None, 'space'), may hold values from 0.05 to 0.45
- thermal_anomaly: float32 [2, 256, 256], P(None, ('space', 'tracer')), may hold values from 0.8 to 1.2
- radiant_flux: float32 [2, 256, 256], P(None, ('space', 'tracer')), may hold values from 0.2 to 1
- daylight_mask: int32 [2, 256, 2], P(None, ('space', 'tracer')), may hold values from 0 to 1, as said below
- baseline_kinetic_coefficient: float32 [768], replicated, may hold values from 0.02 to 1
- arrhenius_barrier: float32 [768], replicated, may hold values from 0.5 to 3
- photodissociation_factor: float32 [768], replicated, may hold values from 0.02 to 1
- stoichiometry_table: int32 [3, 768], replicated, may hold values from 0 to 255
Outputs:
- result: float32 [256, 2, 256, 256], P(None, None, ('space', 'tracer'))
Inputs may be any that keep to these rules, and one draw needn't show every extreme that they name: For every level l, row x below 128 and block b, daylight_mask[l, x, b] + daylight_mask[l, x + 128, b] == 1: a block and the block 128 rows further along the first dimension are never both sunlit or both dark.
All inputs are finite; a program needn't handle non-finite values.
Results may differ from a plain program's by a relative error of at most 0.0003.
Values sent between devices are 32-bit elements; how exact they have to be, the bound alone decides.
A program may use at most 64 MiB of HBM per device.

v0:
```python
import functools

import jax
import jax.numpy as jnp
from jax import lax
from jax.experimental import pallas as pl
from jax.experimental.pallas import tpu as pltpu
from jax.sharding import PartitionSpec as P

MESH = pl.DeviceIdType.MESH
F32 = jnp.float32

SECTIONS = 3
DAY_STEPS = 2
LOW, HIGH = 2 * SECTIONS, SECTIONS
GROUP = 8


def minmod(a, b):
    return jnp.maximum(jnp.minimum(a, jnp.maximum(b, 0.0)), jnp.minimum(b, 0.0))


def transport_kernel(
    strips,
    groups,
    field,
    ux,
    uy,
    uz,
    warm,
    glow,
    base,
    barrier_coef,
    photo,
    cells_out,
    rates_out,
    raw,
    first,
    second,
    third,
    turned,
    packed,
    coef,
    plain,
    edge_up,
    edge_down,
    got_low,
    got_high,
    rates,
    load_sem,
    halo_send,
    halo_recv,
    edge_send,
    edge_recv,
    all_send,
    all_recv,
    own_sem,
    rate_sem,
):
    s = lax.axis_index("space")
    t = lax.axis_index("tracer")
    n_groups = first.shape[0]
    rows = 16
    species_here = n_groups * GROUP
    has_low = s > 0
    has_high = s < strips - 1
    low, high = s - 1, s + 1

    def load(g, blk):
        return pltpu.make_async_copy(
            field.at[pl.ds(g * GROUP, GROUP), :, :, pl.ds(blk * 128, 128)],
            raw.at[blk, pl.ds(g * GROUP, GROUP)],
            load_sem.at[g, blk],
        )

    for g in range(n_groups):
        for blk in range(2):
            load(g, blk).start()

    door = pltpu.get_barrier_semaphore()
    for i in range(1, groups):
        pl.semaphore_signal(
            door, inc=1, device_id=(s, lax.rem(t + i, groups)), device_id_type=MESH
        )

    @pl.when(has_low)
    def _():
        pl.semaphore_signal(door, inc=1, device_id=(low, t), device_id_type=MESH)

    @pl.when(has_high)
    def _():
        pl.semaphore_signal(door, inc=1, device_id=(high, t), device_id_type=MESH)

    for q, u in enumerate((ux, uy, uz)):
        for blk in range(2):
            for l in range(2):
                plain[q, l, blk] = u[l, :, blk * 128 : blk * 128 + 128]
                edge_up[q, blk, l * 4 : l * 4 + 4] = u[l, rows - 4 : rows, blk * 128 : blk * 128 + 128]
                edge_down[q, blk, l * 4 : l * 4 + 4] = u[l, 0:4, blk * 128 : blk * 128 + 128]

    flat = raw.reshape(2 * species_here * 2 * rows, 128)

    def turn(g, row):
        for l in range(2):
            for blk in range(2):
                start = blk * (species_here * 2 * rows) + g * (GROUP * 2 * rows) + l * rows + row
                first[g, row + LOW, l, blk] = flat[pl.ds(start, GROUP, stride=2 * rows), :]

    pl.semaphore_wait(door, groups - 1 + jnp.where(has_low, 1, 0) + jnp.where(has_high, 1, 0))

    def halo_up(g):
        return pltpu.make_async_remote_copy(
            src_ref=first.at[g, pl.ds(rows, LOW)],
            dst_ref=first.at[g, pl.ds(0, LOW)],
            send_sem=halo_send.at[0, g],
            recv_sem=halo_recv.at[0, g],
            device_id=(high, t),
            device_id_type=MESH,
        )

    def halo_down(g):
        return pltpu.make_async_remote_copy(
            src_ref=first.at[g, pl.ds(LOW, HIGH)],
            dst_ref=first.at[g, pl.ds(LOW + rows, HIGH)],
            send_sem=halo_send.at[1, g],
            recv_sem=halo_recv.at[1, g],
            device_id=(low, t),
            device_id_type=MESH,
        )

    def coef_up():
        return pltpu.make_async_remote_copy(
            src_ref=edge_up,
            dst_ref=got_low,
            send_sem=edge_send.at[0],
            recv_sem=edge_recv.at[0],
            device_id=(high, t),
            device_id_type=MESH,
        )

    def coef_down():
        return pltpu.make_async_remote_copy(
            src_ref=edge_down,
            dst_ref=got_high,
            send_sem=edge_send.at[1],
            recv_sem=edge_recv.at[1],
            device_id=(low, t),
            device_id_type=MESH,
        )

    @pl.when(has_high)
    def _():
        coef_up().start()

    @pl.when(has_low)
    def _():
        coef_down().start()

    def send_edges(g, carry):
        load(g, 0).wait()
        load(g, 1).wait()
        for row in range(rows - LOW, rows):
            turn(g, row)

        @pl.when(has_high)
        def _():
            halo_up(g).start()

        for row in range(HIGH):
            turn(g, row)

        @pl.when(has_low)
        def _():
            halo_down(g).start()

        return carry

    lax.fori_loop(0, n_groups, send_edges, 0)

    def turn_rest(g, carry):
        for row in range(HIGH, rows - LOW):
            turn(g, row)
        return carry

    lax.fori_loop(0, n_groups, turn_rest, 0)

    zero = jnp.zeros((GROUP, 128), F32)

    @pl.when(jnp.logical_not(has_low))
    def _():
        for g in range(n_groups):
            for row in range(LOW):
                for l in range(2):
                    for blk in range(2):
                        first[g, row, l, blk] = zero
        for q in range(3):
            for blk in range(2):
                got_low[q, blk] = zero

    @pl.when(jnp.logical_not(has_high))
    def _():
        for g in range(n_groups):
            for row in range(HIGH):
                for l in range(2):
                    for blk in range(2):
                        first[g, LOW + rows + row, l, blk] = zero
        for q in range(3):
            for blk in range(2):
                got_high[q, blk] = zero

    lane = lax.broadcasted_iota(jnp.int32, (GROUP, 128), 1)
    is_first = lane == 0
    is_last = lane == 127

    def from_left(x0, x1):
        r0, r1 = pltpu.roll(x0, 1, 1), pltpu.roll(x1, 1, 1)
        return jnp.where(is_first, r1, r0), jnp.where(is_first, r0, r1)

    def from_right(x0, x1):
        r0, r1 = pltpu.roll(x0, 127, 1), pltpu.roll(x1, 127, 1)
        return jnp.where(is_last, r1, r0), jnp.where(is_last, r0, r1)

    def spread(row, get):
        for l in range(2):
            for q in range(3):
                pair = [jnp.broadcast_to(get(q, l, blk), (GROUP, 128)) for blk in range(2)]
                if q == 1:
                    pair = from_right(*pair)
                for blk in range(2):
                    coef[2 * q, row, l, blk] = pair[blk]
                    coef[2 * q + 1, row, l, blk] = 0.5 * (1.0 - pair[blk])

    def spread_own(row, carry):
        spread(row + 4, lambda q, l, blk: plain[q, l, blk, pl.ds(row, 1), :])
        return carry

    lax.fori_loop(0, rows, spread_own, 0)

    @pl.when(has_low)
    def _():
        coef_up().wait_recv()

    @pl.when(has_high)
    def _():
        coef_down().wait_recv()

    for i in range(4):
        spread(i, lambda q, l, blk: got_low[q, blk, l * 4 + i : l * 4 + i + 1])
    for i in range(3):
        spread(rows + 4 + i, lambda q, l, blk: got_high[q, blk, l * 4 + i : l * 4 + i + 1])

    four = [(l, blk) for l in range(2) for blk in range(2)]

    def one_step(read, lo, count, write):
        state = []
        for l, blk in four:
            c0, c1, c2 = read(lo - 2, l, blk), read(lo - 1, l, blk), read(lo, l, blk)
            d1, d2 = c1 - c0, c2 - c1
            flux = coef[0, lo + 4, l, blk] * (c1 + coef[1, lo + 4, l, blk] * minmod(d1, d2))
            state += [c2, d2, flux]

        def body(i, state):
            row = i + lo
            after, swept = [], []
            for n, (l, blk) in enumerate(four):
                c, d, flux = state[3 * n : 3 * n + 3]
                c_next = read(row + 1, l, blk)
                d_next = c_next - c
                flux_next = coef[0, row + 5, l, blk] * (
                    c + coef[1, row + 5, l, blk] * minmod(d, d_next)
                )
                swept.append(c - (flux_next - flux))
                after += [c_next, d_next, flux_next]
            for l in range(2):
                c0, c1 = swept[2 * l], swept[2 * l + 1]
                m0, m1 = from_left(c0, c1)
                d0, d1 = c0 - m0, c1 - m1
                e0, e1 = from_right(d0, d1)
                g0 = coef[2, row + 4, l, 0] * (c0 + coef[3, row + 4, l, 0] * minmod(d0, e0))
                g1 = coef[2, row + 4, l, 1] * (c1 + coef[3, row + 4, l, 1] * minmod(d1, e1))
                h0, h1 = from_left(g0, g1)
                swept[2 * l] = c0 - (g0 - h0)
                swept[2 * l + 1] = c1 - (g1 - h1)
            for blk in range(2):
                c0, c1 = swept[blk], swept[2 + blk]
                rise = c1 - c0
                g0 = coef[4, row + 4, 0, blk] * (c0 + coef[5, row + 4, 0, blk] * minmod(c0, rise))
                g1 = coef[4, row + 4, 1, blk] * (c1 + coef[5, row + 4, 1, blk] * minmod(rise, -c1))
                write(row, 0, blk, c0 - g0)
                write(row, 1, blk, c1 - (g1 - g0))
            return tuple(after)

        lax.fori_loop(0, count, body, tuple(state))

    def all_copy(g, i):
        to = lax.rem(t + i, groups)
        return pltpu.make_async_remote_copy(
            src_ref=packed.at[g, to],
            dst_ref=cells_out.at[pl.ds(t * species_here + g * GROUP, GROUP)],
            send_sem=all_send.at[g, i - 1],
            recv_sem=all_recv.at[g, i - 1],
            device_id=(s, to),
            device_id_type=MESH,
        )

    def own_copy(g):
        return pltpu.make_async_copy(
            packed.at[g, t],
            cells_out.at[pl.ds(t * species_here + g * GROUP, GROUP)],
            own_sem.at[g],
        )

    turned_flat = turned.reshape(groups * 8 * GROUP, 128)
    order = [i for i in range(1, groups) if i % 2 == 1] + [i for i in range(1, groups) if i % 2 == 0]

    def sweep_group(g, carry):
        @pl.when(has_low)
        def _():
            halo_up(g).wait_recv()

        @pl.when(has_high)
        def _():
            halo_down(g).wait_recv()

        def put2(row, l, blk, v):
            second[row + 4, l, blk] = v

        def put3(row, l, blk, v):
            third[row + 2, l, blk] = v

        def put4(row, l, blk, v):
            turned[row // 2, l * 4 + blk * 2 + row % 2] = v

        one_step(lambda row, l, blk: first[g, row + LOW, l, blk], -4, rows + 6, put2)
        one_step(lambda row, l, blk: second[row + 4, l, blk], -2, rows + 3, put3)
        one_step(lambda row, l, blk: third[row + 2, l, blk], 0, rows, put4)

        def pack(to, carry):
            for k in range(GROUP):
                packed[g, to, k] = turned_flat[pl.ds(to * (8 * GROUP) + k, 8, stride=GROUP), :]
            return carry

        lax.fori_loop(0, groups, pack, 0)
        for i in order:
            all_copy(g, i).start()
        own_copy(g).start()
        return carry

    lax.fori_loop(0, n_groups, sweep_group, 0)

    cold = 1.0 - warm[...]
    light = glow[...]
    reactions = rates.shape[0]

    def rate(i, carry):
        for j in range(8):
            r = i * 8 + j
            rates[r] = base[r] * jnp.exp(barrier_coef[r] * cold) + photo[r] * light
        return carry

    lax.fori_loop(0, reactions // 8, rate, 0)
    rate_copy = pltpu.make_async_copy(rates, rates_out, rate_sem)
    rate_copy.start()

    @pl.when(has_high)
    def _():
        coef_up().wait_send()

    @pl.when(has_low)
    def _():
        coef_down().wait_send()

    def finish(g, carry):
        @pl.when(has_high)
        def _():
            halo_up(g).wait_send()

        @pl.when(has_low)
        def _():
            halo_down(g).wait_send()

        own_copy(g).wait()
        for i in order:
            all_copy(g, i).wait_send()
            source = lax.rem(t + groups - i, groups)
            pltpu.make_async_remote_copy(
                src_ref=packed.at[g, source],
                dst_ref=cells_out.at[pl.ds(source * species_here + g * GROUP, GROUP)],
                send_sem=all_send.at[g, i - 1],
                recv_sem=all_recv.at[g, i - 1],
                device_id=(s, source),
                device_id_type=MESH,
            ).wait_recv()
        return carry

    lax.fori_loop(0, n_groups, finish, 0)
    rate_copy.wait()


def chemistry_kernel(reactions, table, cells, rates, lit, out, *scratch):
    made, lost_a, lost_b, middle = scratch[0:2], scratch[2:4], scratch[4:6], scratch[6]
    species = cells.shape[0] // 8
    zero = jnp.zeros((8, 128), F32)
    sums = (*made, *lost_a, *lost_b)
    at8 = lambda i: pl.ds(pl.multiple_of(i, 8), 8)
    day = lit[...]
    steps = (1.0 - 0.5 * day, 0.5 * day)

    def clear(i, carry):
        for j in range(8):
            for ref in sums:
                ref[at8(i * 64 + j * 8), :] = zero
        return carry

    lax.fori_loop(0, species // 8, clear, 0)
    for number in range(DAY_STEPS):
        source = cells if number == 0 else middle
        target = middle if number == 0 else out
        h = steps[number]

        def react(i, carry):
            for j in range(0, 16, 2):
                new = []
                for k in range(2):
                    r = i * 16 + j + k
                    a, b, p = at8(table[r]), at8(table[reactions + r]), at8(table[2 * reactions + r])
                    rate = rates[at8(r * 8), :]
                    ca, cb = source[a, :], source[b, :]
                    by_a = rate * cb
                    new.append((made[k], p, made[k][p, :] + by_a * ca))
                    new.append((lost_a[k], a, lost_a[k][a, :] + by_a))
                    new.append((lost_b[k], b, lost_b[k][b, :] + rate * ca))
                for ref, where, value in new:
                    ref[where, :] = value
            return carry

        lax.fori_loop(0, reactions // 16, react, 0)

        def update(i, carry):
            for j in range(8):
                o = at8(i * 64 + j * 8)
                gain = made[0][o, :] + made[1][o, :]
                loss = (lost_a[0][o, :] + lost_a[1][o, :]) + (lost_b[0][o, :] + lost_b[1][o, :])
                target[o, :] = (source[o, :] + h * gain) / (1.0 + h * loss)
                if number < DAY_STEPS - 1:
                    for ref in sums:
                        ref[o, :] = zero
            return carry

        lax.fori_loop(0, species // 8, update, 0)


def body(
    strips,
    groups,
    mixing_ratio_field,
    eastward_face_cfl,
    northward_face_cfl,
    upward_face_cfl,
    thermal_anomaly,
    radiant_flux,
    daylight_mask,
    baseline_kinetic_coefficient,
    arrhenius_barrier,
    photodissociation_factor,
    stoichiometry_table,
):
    species_here, levels, rows, width = mixing_ratio_field.shape
    species = species_here * groups
    reactions = baseline_kinetic_coefficient.shape[0]
    n_groups = species_here // GROUP

    def eight(x):
        return x.reshape(2, 2, 2, 128).transpose(0, 2, 1, 3).reshape(8, 128)

    lit = jnp.broadcast_to(
        daylight_mask.transpose(0, 2, 1).reshape(8, 1).astype(F32), (8, 128)
    )
    vmem = pl.BlockSpec(memory_space=pltpu.VMEM)
    smem = pl.BlockSpec(memory_space=pltpu.SMEM)
    anywhere = pl.BlockSpec(memory_space=pl.ANY)
    dma = pltpu.SemaphoreType.DMA
    cells, rates = pl.pallas_call(
        functools.partial(transport_kernel, strips, groups),
        out_shape=(
            jax.ShapeDtypeStruct((species, 8, 128), F32),
            jax.ShapeDtypeStruct((reactions, 8, 128), F32),
        ),
        in_specs=[anywhere, vmem, vmem, vmem, vmem, vmem, smem, smem, smem],
        out_specs=(anywhere, anywhere),
        scratch_shapes=[
            pltpu.VMEM((2, species_here, 2, rows, 128), F32),
            pltpu.VMEM((n_groups, rows + LOW + HIGH, 2, 2, GROUP, 128), F32),
            pltpu.VMEM((rows + 6, 2, 2, GROUP, 128), F32),
            pltpu.VMEM((rows + 3, 2, 2, GROUP, 128), F32),
            pltpu.VMEM((groups, 8, GROUP, 128), F32),
            pltpu.VMEM((n_groups, groups, GROUP, 8, 128), F32),
            pltpu.VMEM((6, rows + 7, 2, 2, GROUP, 128), F32),
            pltpu.VMEM((3, 2, 2, rows, 128), F32),
            pltpu.VMEM((3, 2, 8, 128), F32),
            pltpu.VMEM((3, 2, 8, 128), F32),
            pltpu.VMEM((3, 2, 8, 128), F32),
            pltpu.VMEM((3, 2, 8, 128), F32),
            pltpu.VMEM((reactions, 8, 128), F32),
            dma((n_groups, 2)),
            dma((2, n_groups)),
            dma((2, n_groups)),
            dma((2,)),
            dma((2,)),
            dma((n_groups, groups - 1)),
            dma((n_groups, groups - 1)),
            dma((n_groups,)),
            dma,
        ],
        compiler_params=pltpu.CompilerParams(
            collective_id=0, has_side_effects=True, vmem_limit_bytes=24 << 20
        ),
        name="transport",
    )(
        mixing_ratio_field,
        eastward_face_cfl,
        northward_face_cfl,
        upward_face_cfl,
        eight(thermal_anomaly),
        eight(radiant_flux) * lit,
        baseline_kinetic_coefficient,
        arrhenius_barrier,
        photodissociation_factor,
    )
    out = pl.pallas_call(
        functools.partial(chemistry_kernel, reactions),
        out_shape=jax.ShapeDtypeStruct((species * 8, 128), F32),
        in_specs=[smem, vmem, vmem, vmem],
        out_specs=vmem,
        scratch_shapes=[pltpu.VMEM((species * 8, 128), F32)] * 7,
        compiler_params=pltpu.CompilerParams(vmem_limit_bytes=24 << 20),
        name="chemistry",
    )(
        (stoichiometry_table * 8).reshape(3 * reactions),
        cells.reshape(species * 8, 128),
        rates.reshape(reactions * 8, 128),
        lit,
    )
    return out.reshape(species, 2, 2, 2, 128).transpose(0, 1, 3, 2, 4).reshape(species, 2, 2, 256)


def solution(mesh):
    placed = (
        P("tracer", None, "space", None),
        P(None, "space", None),
        P(None, "space", None),
        P(None, "space", None),
        P(None, ("space", "tracer"), None),
        P(None, ("space", "tracer"), None),
        P(None, ("space", "tracer"), None),
        P(),
        P(),
        P(),
        P(),
    )
    return jax.shard_map(
        functools.partial(body, mesh.shape["space"], mesh.shape["tracer"]),
        mesh=mesh,
        in_specs=placed,
        out_specs=P(None, None, ("space", "tracer"), None),
        check_vma=False,
    )
```

profile of v0, /device:TPU:64, one launch (start us, length us, event | category | flops | bytes accessed | tf_op | source)
XLA Modules:
  0.0 88.6 jit_solution(1619959630212416120)
XLA Ops:
  0.0 0.7 convert_bitcast_fusion
  0.7 0.1 copy.14
  0.8 0.1 convert_element_type.16
  0.9 0.8 broadcast_multiply_fusion.1.glow
  1.6 0.1 broadcast_in_dim.2.lit
  1.7 0.7 broadcast_multiply_fusion
  2.4 0.0 copy-start
  2.4 1.2 %copy-done = f32[32,2,16,256]{3,2,1,0:T(8,128)S(1)} copy-done((f32[32,2,16,256]{3,2,1,0:T(8,128)S(1)}, f32[32,2,16,256]{3,2,1,0:T(8,128)}, u32[]{:S(2)}) %copy-start) | copy-done | bytes 1048600
  3.6 0.0 copy-start.1
  3.6 0.8 copy-done.1
  4.4 0.0 copy-start.2
  4.4 0.8 copy-done.2
  5.2 0.0 copy-start.3
  5.2 0.8 copy-done.3
  5.9 0.0 copy-start.4
  5.9 0.7 copy-done.4
  6.6 0.0 copy-start.5
  6.6 0.7 copy-done.5
  7.3 0.0 copy-start.6
  7.3 0.7 copy-done.6
  8.0 0.0 copy-start.7
  8.0 0.7 copy-done.7
  8.7 71.3 %transport.1 = (f32[256,8,128]{2,1,0:T(8,128)S(1)}, f32[768,8,128]{2,1,0:T(8,128)S(1)}) custom-call(f32[32,2,16,256]{3,2,1,0:T(8,128)S(1)} %copy-done, f32[2,16,256]{2,1,0:T(8,128)S(1)} %copy-done.1, f32[2,16,256]{2,1,0:T(8,128)S(1)} %copy-done.2, f32[2,16,256]{2,1,0:T(8,128)S(1)} %copy-done.3, f32[8,128]{1,0:T(8,128)S(1)} %bitcast.21, ...), custom_call_target="tpu_custom_call" | custom-call | tf_op jit(solution)/shard_map/transport/pallas_call | solution.py:483
  80.0 8.6 %chemistry.1 = f32[2048,128]{1,0:T(8,128)} custom-call(s32[2304]{0:T(1024)S(1)} %reshape.36.table, f32[2048,128]{1,0:T(8,128)S(1)} %bitcast.20, f32[6144,128]{1,0:T(8,128)S(1)} %bitcast.19, f32[8,128]{1,0:T(8,128)S(1)} %broadcast_in_dim.2.lit), custom_call_target="tpu_custom_call" | custom-call | tf_op jit(solution)/shard_map/chemistry/pallas_call | solution.py:530
  (1 shorter events, 0.0 us)
Async XLA Ops:
  2.4 1.2 %copy-start = (f32[32,2,16,256]{3,2,1,0:T(8,128)S(1)}, f32[32,2,16,256]{3,2,1,0:T(8,128)}, u32[]{:S(2)}) copy-start(f32[32,2,16,256]{3,2,1,0:T(8,128)} %field.1) | copy-start | bytes 3145732
  3.6 0.8 copy-start.1
  4.4 0.8 copy-start.2
  5.2 0.8 copy-start.3
  5.9 0.7 copy-start.4
  6.6 0.7 copy-start.5
  7.3 0.7 copy-start.6
  8.0 0.7 copy-start.7
where the time goes:
time: 89.2 us; the launch traced here: 88.6 us
  Pallas kernels  80 us (90%)
  local copies, waits for them, and re-layouts  6.5 us (7%)
  other arithmetic  2.15 us (2%)
    pallas_call x1, Pallas kernels, body(): pl.pallas_call(functools.partial(transport_kernel, strips, groups), out_s...  71.3 us
    pallas_call x1, Pallas kernels, body(): pl.pallas_call(functools.partial(chemistry_kernel, reactions), out_shape=...  8.62 us
    unnamed x16, local copies, waits for them, and re-layouts  6.24 us

commit v1 on v0

--- a/solution.py
+++ b/solution.py
@@ -13,6 +13,10 @@
 SECTIONS = 3
 DAY_STEPS = 2
 LOW, HIGH = 2 * SECTIONS, SECTIONS
+UNROLL = 11
+VMEM_BYTES = 60 << 20
+CHUNKS = 6
+PIECES = 4
 GROUP = 8
 
 
@@ -29,11 +33,15 @@
     uz,
     warm,
     glow,
+    mask,
     base,
     barrier_coef,
     photo,
+    stoichiometry,
     cells_out,
     rates_out,
+    table_out,
+    lit_out,
     raw,
     first,
     second,
@@ -47,7 +55,14 @@
     got_low,
     got_high,
     rates,
+    sky,
+    mask_here,
+    coefs,
+    species_of,
+    table,
     load_sem,
+    plain_sem,
+    small_sem,
     halo_send,
     halo_recv,
     edge_send,
@@ -77,6 +92,30 @@
         for blk in range(2):
             load(g, blk).start()
 
+    plain_in = [
+        pltpu.make_async_copy(
+            u.at[:, :, pl.ds(blk * 128, 128)], plain.at[q, blk], plain_sem.at[q, blk]
+        )
+        for q, u in enumerate((ux, uy, uz))
+        for blk in range(2)
+    ]
+    small_in = [
+        pltpu.make_async_copy(source, target, small_sem.at[i])
+        for i, (source, target) in enumerate(
+            (
+                (warm, sky.at[0]),
+                (glow, sky.at[1]),
+                (mask, mask_here),
+                (stoichiometry, species_of),
+                (base, coefs.at[pl.ds(0, base.shape[0])]),
+                (barrier_coef, coefs.at[pl.ds(1024, base.shape[0])]),
+                (photo, coefs.at[pl.ds(2048, base.shape[0])]),
+            )
+        )
+    ]
+    for copy in plain_in + small_in:
+        copy.start()
+
     door = pltpu.get_barrier_semaphore()
     for i in range(1, groups):
         pl.semaphore_signal(
@@ -91,12 +130,13 @@
     def _():
         pl.semaphore_signal(door, inc=1, device_id=(high, t), device_id_type=MESH)
 
-    for q, u in enumerate((ux, uy, uz)):
+    for copy in plain_in:
+        copy.wait()
+    for q in range(3):
         for blk in range(2):
             for l in range(2):
-                plain[q, l, blk] = u[l, :, blk * 128 : blk * 128 + 128]
-                edge_up[q, blk, l * 4 : l * 4 + 4] = u[l, rows - 4 : rows, blk * 128 : blk * 128 + 128]
-                edge_down[q, blk, l * 4 : l * 4 + 4] = u[l, 0:4, blk * 128 : blk * 128 + 128]
+                edge_up[q, blk, l * 4 : l * 4 + 4] = plain[q, blk, l, rows - 4 : rows]
+                edge_down[q, blk, l * 4 : l * 4 + 4] = plain[q, blk, l, 0:4]
 
     flat = raw.reshape(2 * species_here * 2 * rows, 128)
 
@@ -231,7 +271,7 @@
                     coef[2 * q + 1, row, l, blk] = 0.5 * (1.0 - pair[blk])
 
     def spread_own(row, carry):
-        spread(row + 4, lambda q, l, blk: plain[q, l, blk, pl.ds(row, 1), :])
+        spread(row + 4, lambda q, l, blk: plain[q, blk, l, pl.ds(row, 1), :])
         return carry
 
     lax.fori_loop(0, rows, spread_own, 0)
@@ -290,7 +330,14 @@
                 write(row, 1, blk, c1 - (g1 - g0))
             return tuple(after)
 
-        lax.fori_loop(0, count, body, tuple(state))
+        def several(n, state):
+            for j in range(UNROLL):
+                state = body(n * UNROLL + j, state)
+            return state
+
+        state = lax.fori_loop(0, count // UNROLL, several, tuple(state))
+        for j in range(count - count % UNROLL, count):
+            state = body(j, state)
 
     def all_copy(g, i):
         to = lax.rem(t + i, groups)
@@ -348,19 +395,32 @@
 
     lax.fori_loop(0, n_groups, sweep_group, 0)
 
-    cold = 1.0 - warm[...]
-    light = glow[...]
+    for copy in small_in:
+        copy.wait()
+    for l in range(2):
+        for blk in range(2):
+            lit_out[l * 4 + blk * 2 : l * 4 + blk * 2 + 2, :] = jnp.broadcast_to(
+                mask_here[l, :, blk : blk + 1].astype(F32), (2, 128)
+            )
+    cold = 1.0 - sky[0]
+    light = sky[1] * lit_out[...]
     reactions = rates.shape[0]
+    for q in range(3):
+        for j in range(reactions // 128):
+            n = q * (reactions // 128) + j
+            table[n : n + 1, :] = species_of[q : q + 1, j * 128 : j * 128 + 128] * 8
 
     def rate(i, carry):
         for j in range(8):
             r = i * 8 + j
-            rates[r] = base[r] * jnp.exp(barrier_coef[r] * cold) + photo[r] * light
+            rates[r] = coefs[r] * jnp.exp(coefs[1024 + r] * cold) + coefs[2048 + r] * light
         return carry
 
     lax.fori_loop(0, reactions // 8, rate, 0)
-    rate_copy = pltpu.make_async_copy(rates, rates_out, rate_sem)
+    rate_copy = pltpu.make_async_copy(rates, rates_out, rate_sem.at[0])
     rate_copy.start()
+    table_copy = pltpu.make_async_copy(table, table_out, rate_sem.at[1])
+    table_copy.start()
 
     @pl.when(has_high)
     def _():
@@ -395,16 +455,51 @@
 
     lax.fori_loop(0, n_groups, finish, 0)
     rate_copy.wait()
-
-
-def chemistry_kernel(reactions, table, cells, rates, lit, out, *scratch):
-    made, lost_a, lost_b, middle = scratch[0:2], scratch[2:4], scratch[4:6], scratch[6]
+    table_copy.wait()
+
+
+def chemistry_kernel(
+    reactions,
+    table_in,
+    cells_in,
+    rates_in,
+    lit_in,
+    out,
+    table,
+    cells,
+    rates,
+    lit,
+    result,
+    made_0,
+    made_1,
+    lost_a0,
+    lost_a1,
+    lost_b0,
+    lost_b1,
+    middle,
+    first_sem,
+    rate_sem,
+    out_sem,
+):
+    made, lost_a, lost_b = (made_0, made_1), (lost_a0, lost_a1), (lost_b0, lost_b1)
     species = cells.shape[0] // 8
     zero = jnp.zeros((8, 128), F32)
     sums = (*made, *lost_a, *lost_b)
     at8 = lambda i: pl.ds(pl.multiple_of(i, 8), 8)
-    day = lit[...]
-    steps = (1.0 - 0.5 * day, 0.5 * day)
+    first_in = [
+        pltpu.make_async_copy(source, target, first_sem.at[i])
+        for i, (source, target) in enumerate(((cells_in, cells), (table_in, table), (lit_in, lit)))
+    ]
+    part = reactions // CHUNKS
+
+    def rates_piece(i):
+        where = pl.ds(pl.multiple_of(i * part * 8, 8), part * 8)
+        return pltpu.make_async_copy(rates_in.at[where, :], rates.at[where, :], rate_sem.at[i])
+
+    for copy in first_in:
+        copy.start()
+    for i in range(CHUNKS):
+        rates_piece(i).start()
 
     def clear(i, carry):
         for j in range(8):
@@ -413,9 +508,20 @@
         return carry
 
     lax.fori_loop(0, species // 8, clear, 0)
+    for copy in first_in:
+        copy.wait()
+    day = lit[...]
+    steps = (1.0 - 0.5 * day, 0.5 * day)
+    piece = species // PIECES
+
+    def out_piece(i):
+        where = pl.ds(pl.multiple_of(i * piece * 8, 8), piece * 8)
+        return pltpu.make_async_copy(result.at[where, :], out.at[where, :], out_sem.at[i])
+
     for number in range(DAY_STEPS):
+        last = number == DAY_STEPS - 1
         source = cells if number == 0 else middle
-        target = middle if number == 0 else out
+        target = result if last else middle
         h = steps[number]
 
         def react(i, carry):
@@ -434,7 +540,15 @@
                     ref[where, :] = value
             return carry
 
-        lax.fori_loop(0, reactions // 16, react, 0)
+        if number == 0:
+
+            def react_chunk(i, carry):
+                rates_piece(i).wait()
+                return lax.fori_loop(i * (part // 16), (i + 1) * (part // 16), react, carry)
+
+            lax.fori_loop(0, CHUNKS, react_chunk, 0)
+        else:
+            lax.fori_loop(0, reactions // 16, react, 0)
 
         def update(i, carry):
             for j in range(8):
@@ -442,12 +556,22 @@
                 gain = made[0][o, :] + made[1][o, :]
                 loss = (lost_a[0][o, :] + lost_a[1][o, :]) + (lost_b[0][o, :] + lost_b[1][o, :])
                 target[o, :] = (source[o, :] + h * gain) / (1.0 + h * loss)
-                if number < DAY_STEPS - 1:
+                if not last:
                     for ref in sums:
                         ref[o, :] = zero
             return carry
 
-        lax.fori_loop(0, species // 8, update, 0)
+        def update_piece(i, carry):
+            lax.fori_loop(i * (piece // 8), (i + 1) * (piece // 8), update, 0)
+            out_piece(i).start()
+            return carry
+
+        if last:
+            lax.fori_loop(0, PIECES, update_piece, 0)
+        else:
+            lax.fori_loop(0, species // 8, update, 0)
+    for i in range(PIECES):
+        out_piece(i).wait()
 
 
 def body(
@@ -473,21 +597,19 @@
     def eight(x):
         return x.reshape(2, 2, 2, 128).transpose(0, 2, 1, 3).reshape(8, 128)
 
-    lit = jnp.broadcast_to(
-        daylight_mask.transpose(0, 2, 1).reshape(8, 1).astype(F32), (8, 128)
-    )
     vmem = pl.BlockSpec(memory_space=pltpu.VMEM)
-    smem = pl.BlockSpec(memory_space=pltpu.SMEM)
-    anywhere = pl.BlockSpec(memory_space=pl.ANY)
+    hbm = pl.BlockSpec(memory_space=pltpu.HBM)
     dma = pltpu.SemaphoreType.DMA
-    cells, rates = pl.pallas_call(
+    cells, rates, table, lit = pl.pallas_call(
         functools.partial(transport_kernel, strips, groups),
         out_shape=(
             jax.ShapeDtypeStruct((species, 8, 128), F32),
             jax.ShapeDtypeStruct((reactions, 8, 128), F32),
+            jax.ShapeDtypeStruct((24, 128), jnp.int32),
+            jax.ShapeDtypeStruct((8, 128), F32),
         ),
-        in_specs=[anywhere, vmem, vmem, vmem, vmem, vmem, smem, smem, smem],
-        out_specs=(anywhere, anywhere),
+        in_specs=[hbm] * 11,
+        out_specs=(hbm, hbm, hbm, vmem),
         scratch_shapes=[
             pltpu.VMEM((2, species_here, 2, rows, 128), F32),
             pltpu.VMEM((n_groups, rows + LOW + HIGH, 2, 2, GROUP, 128), F32),
@@ -502,7 +624,14 @@
             pltpu.VMEM((3, 2, 8, 128), F32),
             pltpu.VMEM((3, 2, 8, 128), F32),
             pltpu.VMEM((reactions, 8, 128), F32),
+            pltpu.VMEM((2, 8, 128), F32),
+            pltpu.VMEM((2, 2, 2), jnp.int32),
+            pltpu.SMEM((3 * 1024,), F32),
+            pltpu.VMEM((3, reactions), jnp.int32),
+            pltpu.VMEM((24, 128), jnp.int32),
             dma((n_groups, 2)),
+            dma((3, 2)),
+            dma((7,)),
             dma((2, n_groups)),
             dma((2, n_groups)),
             dma((2,)),
@@ -510,10 +639,10 @@
             dma((n_groups, groups - 1)),
             dma((n_groups, groups - 1)),
             dma((n_groups,)),
-            dma,
+            dma((2,)),
         ],
         compiler_params=pltpu.CompilerParams(
-            collective_id=0, has_side_effects=True, vmem_limit_bytes=24 << 20
+            collective_id=0, has_side_effects=True, vmem_limit_bytes=VMEM_BYTES
         ),
         name="transport",
     )(
@@ -522,21 +651,30 @@
         northward_face_cfl,
         upward_face_cfl,
         eight(thermal_anomaly),
-        eight(radiant_flux) * lit,
+        eight(radiant_flux),
+        daylight_mask,
         baseline_kinetic_coefficient,
         arrhenius_barrier,
         photodissociation_factor,
+        stoichiometry_table,
     )
     out = pl.pallas_call(
         functools.partial(chemistry_kernel, reactions),
         out_shape=jax.ShapeDtypeStruct((species * 8, 128), F32),
-        in_specs=[smem, vmem, vmem, vmem],
-        out_specs=vmem,
-        scratch_shapes=[pltpu.VMEM((species * 8, 128), F32)] * 7,
-        compiler_params=pltpu.CompilerParams(vmem_limit_bytes=24 << 20),
+        in_specs=[hbm] * 4,
+        out_specs=hbm,
+        scratch_shapes=[
+            pltpu.SMEM((24 * 128,), jnp.int32),
+            pltpu.VMEM((species * 8, 128), F32),
+            pltpu.VMEM((reactions * 8, 128), F32),
+            pltpu.VMEM((8, 128), F32),
+        ]
+        + [pltpu.VMEM((species * 8, 128), F32)] * 8
+        + [dma((3,)), dma((CHUNKS,)), dma((PIECES,))],
+        compiler_params=pltpu.CompilerParams(vmem_limit_bytes=VMEM_BYTES),
         name="chemistry",
     )(
-        (stoichiometry_table * 8).reshape(3 * reactions),
+        table.reshape(24 * 128),
         cells.reshape(species * 8, 128),
         rates.reshape(reactions * 8, 128),
         lit,

time: 89.2 us -> 37.5 us (0.42)
  Pallas kernels: 80 us -> 37.3 us
  local copies, waits for them, and re-layouts: 6.5 us -> 0 us
  other arithmetic: 2.15 us -> 0 us
    pallas_call x1, Pallas kernels: 71.3 us -> 28.2 us  [body(): pl.pallas_call(functools.partial(transport_kernel, strips, groups), out_s...]
    unnamed x16 -> x0, local copies, waits for them, and re-layouts: 6.24 us -> none
    mul x2 -> x0, other arithmetic: 1.47 us -> none  [the longest x1 0.76 us: body(): eight(radiant_flux) * lit]
where the time goes in v1:
time: 37.5 us; the launch traced here: 37.3 us
  Pallas kernels  37.3 us (99%)
    pallas_call x1, Pallas kernels, body(): pl.pallas_call(functools.partial(transport_kernel, strips, groups), out_s...  28.2 us
    pallas_call x1, Pallas kernels, body(): pl.pallas_call(functools.partial(chemistry_kernel, reactions), out_shape=...  9.15 us

profile of v1, /device:TPU:64, one launch (start us, length us, event | category | flops | bytes accessed | tf_op | source)
XLA Modules:
  0.0 37.3 jit_solution(10956022036558507677)
XLA Ops:
  0.0 28.2 %transport.1 = (f32[256,8,128]{2,1,0:T(8,128)}, f32[768,8,128]{2,1,0:T(8,128)}, s32[24,128]{1,0:T(8,128)}, f32[8,128]{1,0:T(8,128)}) custom-call(f32[32,2,16,256]{3,2,1,0:T(8,128)} %field.1, f32[2,16,256]{2,1,0:T(8,128)} %ux.1, f32[2,16,256]{2,1,0:T(8,128)} %uy.1, f32[2,16,256]{2,1,0:T(8,128)} %uz.1, f32[8,128]{1,0:T(8,128)} %bitcast.21, f32[8,128]{1,0:T(8,128)} %bitcast.22, ...), custom_call_target="tpu_custom_call" | custom-call | tf_op jit(solution)/shard_map/transport/pallas_call | solution.py:603
  28.2 9.2 %chemistry.1 = f32[2048,128]{1,0:T(8,128)} custom-call(s32[3072]{0:T(1024)} %bitcast.20, f32[2048,128]{1,0:T(8,128)} %bitcast.19, f32[6144,128]{1,0:T(8,128)} %bitcast.18, f32[8,128]{1,0:T(8,128)} %get-tuple-element.12.lit_in), custom_call_target="tpu_custom_call" | custom-call | tf_op jit(solution)/shard_map/chemistry/pallas_call | solution.py:661

commit v2 on v1

--- a/solution.py
+++ b/solution.py
@@ -13,9 +13,10 @@
 SECTIONS = 3
 DAY_STEPS = 2
 LOW, HIGH = 2 * SECTIONS, SECTIONS
-UNROLL = 11
+UNROLL = 8
 VMEM_BYTES = 60 << 20
-CHUNKS = 6
+ROUND = 4
+CHUNKS = 4
 PIECES = 4
 GROUP = 8
 
@@ -46,7 +47,6 @@
     first,
     second,
     third,
-    turned,
     packed,
     coef,
     plain,
@@ -357,8 +357,19 @@
             own_sem.at[g],
         )
 
-    turned_flat = turned.reshape(groups * 8 * GROUP, 128)
+    packed_flat = packed.reshape(n_groups * groups * GROUP * 8, 128)
     order = [i for i in range(1, groups) if i % 2 == 1] + [i for i in range(1, groups) if i % 2 == 0]
+
+    def halos_gone(g, carry):
+        @pl.when(has_high)
+        def _():
+            halo_up(g).wait_send()
+
+        @pl.when(has_low)
+        def _():
+            halo_down(g).wait_send()
+
+        return carry
 
     def sweep_group(g, carry):
         @pl.when(has_low)
@@ -376,18 +387,17 @@
             third[row + 2, l, blk] = v
 
         def put4(row, l, blk, v):
-            turned[row // 2, l * 4 + blk * 2 + row % 2] = v
+            start = (g * groups + row // 2) * (GROUP * 8) + l * 4 + blk * 2 + row % 2
+            packed_flat[pl.ds(start, GROUP, stride=8), :] = v
 
         one_step(lambda row, l, blk: first[g, row + LOW, l, blk], -4, rows + 6, put2)
         one_step(lambda row, l, blk: second[row + 4, l, blk], -2, rows + 3, put3)
         one_step(lambda row, l, blk: third[row + 2, l, blk], 0, rows, put4)
 
-        def pack(to, carry):
-            for k in range(GROUP):
-                packed[g, to, k] = turned_flat[pl.ds(to * (8 * GROUP) + k, 8, stride=GROUP), :]
-            return carry
-
-        lax.fori_loop(0, groups, pack, 0)
+        @pl.when(g == 0)
+        def _():
+            lax.fori_loop(0, n_groups, halos_gone, 0)
+
         for i in order:
             all_copy(g, i).start()
         own_copy(g).start()
@@ -410,13 +420,18 @@
             n = q * (reactions // 128) + j
             table[n : n + 1, :] = species_of[q : q + 1, j * 128 : j * 128 + 128] * 8
 
+    ways = reactions // 128
+
     def rate(i, carry):
-        for j in range(8):
-            r = i * 8 + j
-            rates[r] = coefs[r] * jnp.exp(coefs[1024 + r] * cold) + coefs[2048 + r] * light
-        return carry
-
-    lax.fori_loop(0, reactions // 8, rate, 0)
+        for j in range(2):
+            for w in range(ways):
+                r = w * 128 + 2 * i + j
+                rates[(2 * i + j) * ways + w] = (
+                    coefs[r] * jnp.exp(coefs[1024 + r] * cold) + coefs[2048 + r] * light
+                )
+        return carry
+
+    lax.fori_loop(0, 128 // 2, rate, 0)
     rate_copy = pltpu.make_async_copy(rates, rates_out, rate_sem.at[0])
     rate_copy.start()
     table_copy = pltpu.make_async_copy(table, table_out, rate_sem.at[1])
@@ -431,14 +446,6 @@
         coef_down().wait_send()
 
     def finish(g, carry):
-        @pl.when(has_high)
-        def _():
-            halo_up(g).wait_send()
-
-        @pl.when(has_low)
-        def _():
-            halo_down(g).wait_send()
-
         own_copy(g).wait()
         for i in order:
             all_copy(g, i).wait_send()
@@ -458,42 +465,25 @@
     table_copy.wait()
 
 
-def chemistry_kernel(
-    reactions,
-    table_in,
-    cells_in,
-    rates_in,
-    lit_in,
-    out,
-    table,
-    cells,
-    rates,
-    lit,
-    result,
-    made_0,
-    made_1,
-    lost_a0,
-    lost_a1,
-    lost_b0,
-    lost_b1,
-    middle,
-    first_sem,
-    rate_sem,
-    out_sem,
-):
-    made, lost_a, lost_b = (made_0, made_1), (lost_a0, lost_a1), (lost_b0, lost_b1)
+def chemistry_kernel(ways, table_in, cells_in, rates_in, lit_in, out, *scratch):
+    cells, rates, lit, result, middle = scratch[:5]
+    sums = scratch[5 : 5 + 6 * DAY_STEPS]
+    table = scratch[5 + 6 * DAY_STEPS : 5 + 6 * DAY_STEPS + 3 * ways]
+    first_sem, table_sem, rate_sem, out_sem = scratch[-4:]
     species = cells.shape[0] // 8
     zero = jnp.zeros((8, 128), F32)
-    sums = (*made, *lost_a, *lost_b)
     at8 = lambda i: pl.ds(pl.multiple_of(i, 8), 8)
     first_in = [
         pltpu.make_async_copy(source, target, first_sem.at[i])
-        for i, (source, target) in enumerate(((cells_in, cells), (table_in, table), (lit_in, lit)))
+        for i, (source, target) in enumerate(((cells_in, cells), (lit_in, lit)))
+    ] + [
+        pltpu.make_async_copy(table_in.at[pl.ds(n * 128, 128)], table[n], table_sem.at[n])
+        for n in range(3 * ways)
     ]
-    part = reactions // CHUNKS
+    part = 128 // CHUNKS
 
     def rates_piece(i):
-        where = pl.ds(pl.multiple_of(i * part * 8, 8), part * 8)
+        where = pl.ds(pl.multiple_of(i * part * ways * 8, 8), part * ways * 8)
         return pltpu.make_async_copy(rates_in.at[where, :], rates.at[where, :], rate_sem.at[i])
 
     for copy in first_in:
@@ -502,12 +492,12 @@
         rates_piece(i).start()
 
     def clear(i, carry):
-        for j in range(8):
+        for j in range(4):
             for ref in sums:
-                ref[at8(i * 64 + j * 8), :] = zero
-        return carry
-
-    lax.fori_loop(0, species // 8, clear, 0)
+                ref[at8(i * 32 + j * 8), :] = zero
+        return carry
+
+    lax.fori_loop(0, species // 4, clear, 0)
     for copy in first_in:
         copy.wait()
     day = lit[...]
@@ -523,32 +513,34 @@
         source = cells if number == 0 else middle
         target = result if last else middle
         h = steps[number]
-
-        def react(i, carry):
-            for j in range(0, 16, 2):
-                new = []
-                for k in range(2):
-                    r = i * 16 + j + k
-                    a, b, p = at8(table[r]), at8(table[reactions + r]), at8(table[2 * reactions + r])
-                    rate = rates[at8(r * 8), :]
-                    ca, cb = source[a, :], source[b, :]
-                    by_a = rate * cb
-                    new.append((made[k], p, made[k][p, :] + by_a * ca))
-                    new.append((lost_a[k], a, lost_a[k][a, :] + by_a))
-                    new.append((lost_b[k], b, lost_b[k][b, :] + rate * ca))
-                for ref, where, value in new:
-                    ref[where, :] = value
+        made, lost_a, lost_b = (sums[6 * number + 2 * n : 6 * number + 2 * n + 2] for n in range(3))
+
+        def react(n, carry):
+            for j in range(ROUND):
+                i = n * ROUND + j
+                for w in range(0, ways, 2):
+                    new = []
+                    for k in range(2):
+                        a, b, p = (at8(table[q * ways + w + k][i]) for q in range(3))
+                        rate = rates[at8(n * (ROUND * ways * 8) + (j * ways + w + k) * 8), :]
+                        ca, cb = source[a, :], source[b, :]
+                        by_a = rate * cb
+                        new.append((made[k], p, made[k][p, :] + by_a * ca))
+                        new.append((lost_a[k], a, lost_a[k][a, :] + by_a))
+                        new.append((lost_b[k], b, lost_b[k][b, :] + rate * ca))
+                    for ref, where, value in new:
+                        ref[where, :] = value
             return carry
 
         if number == 0:
 
             def react_chunk(i, carry):
                 rates_piece(i).wait()
-                return lax.fori_loop(i * (part // 16), (i + 1) * (part // 16), react, carry)
+                return lax.fori_loop(i * (part // ROUND), (i + 1) * (part // ROUND), react, carry)
 
             lax.fori_loop(0, CHUNKS, react_chunk, 0)
         else:
-            lax.fori_loop(0, reactions // 16, react, 0)
+            lax.fori_loop(0, 128 // ROUND, react, 0)
 
         def update(i, carry):
             for j in range(8):
@@ -556,9 +548,6 @@
                 gain = made[0][o, :] + made[1][o, :]
                 loss = (lost_a[0][o, :] + lost_a[1][o, :]) + (lost_b[0][o, :] + lost_b[1][o, :])
                 target[o, :] = (source[o, :] + h * gain) / (1.0 + h * loss)
-                if not last:
-                    for ref in sums:
-                        ref[o, :] = zero
             return carry
 
         def update_piece(i, carry):
@@ -615,7 +604,6 @@
             pltpu.VMEM((n_groups, rows + LOW + HIGH, 2, 2, GROUP, 128), F32),
             pltpu.VMEM((rows + 6, 2, 2, GROUP, 128), F32),
             pltpu.VMEM((rows + 3, 2, 2, GROUP, 128), F32),
-            pltpu.VMEM((groups, 8, GROUP, 128), F32),
             pltpu.VMEM((n_groups, groups, GROUP, 8, 128), F32),
             pltpu.VMEM((6, rows + 7, 2, 2, GROUP, 128), F32),
             pltpu.VMEM((3, 2, 2, rows, 128), F32),
@@ -659,18 +647,18 @@
         stoichiometry_table,
     )
     out = pl.pallas_call(
-        functools.partial(chemistry_kernel, reactions),
+        functools.partial(chemistry_kernel, reactions // 128),
         out_shape=jax.ShapeDtypeStruct((species * 8, 128), F32),
         in_specs=[hbm] * 4,
         out_specs=hbm,
         scratch_shapes=[
-            pltpu.SMEM((24 * 128,), jnp.int32),
             pltpu.VMEM((species * 8, 128), F32),
             pltpu.VMEM((reactions * 8, 128), F32),
             pltpu.VMEM((8, 128), F32),
         ]
-        + [pltpu.VMEM((species * 8, 128), F32)] * 8
-        + [dma((3,)), dma((CHUNKS,)), dma((PIECES,))],
+        + [pltpu.VMEM((species * 8, 128), F32)] * (2 + 6 * DAY_STEPS)
+        + [pltpu.SMEM((128,), jnp.int32)] * (3 * (reactions // 128))
+        + [dma((2,)), dma((3 * (reactions // 128),)), dma((CHUNKS,)), dma((PIECES,))],
         compiler_params=pltpu.CompilerParams(vmem_limit_bytes=VMEM_BYTES),
         name="chemistry",
     )(

time: 37.5 us -> 36.6 us (0.976)
  Pallas kernels: 37.3 us -> 36.2 us
    pallas_call x1, Pallas kernels: 28.2 us -> 27.1 us  [body(): pl.pallas_call(functools.partial(transport_kernel, strips, groups), out_s...]
where the time goes in v2:
time: 36.6 us; the launch traced here: 36.2 us
  Pallas kernels  36.2 us (99%)
    pallas_call x1, Pallas kernels, body(): pl.pallas_call(functools.partial(transport_kernel, strips, groups), out_s...  27.1 us
    pallas_call x1, Pallas kernels, body(): pl.pallas_call(functools.partial(chemistry_kernel, reactions // 128), out...  9.05 us

profile of v2, /device:TPU:64, one launch (start us, length us, event | category | flops | bytes accessed | tf_op | source)
XLA Modules:
  0.0 36.2 jit_solution(2937284233982104944)
XLA Ops:
  0.0 27.1 %transport.1 = (f32[256,8,128]{2,1,0:T(8,128)}, f32[768,8,128]{2,1,0:T(8,128)}, s32[24,128]{1,0:T(8,128)}, f32[8,128]{1,0:T(8,128)}) custom-call(f32[32,2,16,256]{3,2,1,0:T(8,128)} %field.1, f32[2,16,256]{2,1,0:T(8,128)} %ux.1, f32[2,16,256]{2,1,0:T(8,128)} %uy.1, f32[2,16,256]{2,1,0:T(8,128)} %uz.1, f32[8,128]{1,0:T(8,128)} %bitcast.21, f32[8,128]{1,0:T(8,128)} %bitcast.22, ...), custom_call_target="tpu_custom_call" | custom-call | tf_op jit(solution)/shard_map/transport/pallas_call | solution.py:592
  27.1 9.0 %chemistry.1 = f32[2048,128]{1,0:T(8,128)} custom-call(s32[3072]{0:T(1024)} %bitcast.20, f32[2048,128]{1,0:T(8,128)} %bitcast.19, f32[6144,128]{1,0:T(8,128)} %bitcast.18, f32[8,128]{1,0:T(8,128)} %get-tuple-element.12.lit_in), custom_call_target="tpu_custom_call" | custom-call | tf_op jit(solution)/shard_map/chemistry/pallas_call | solution.py:649

commit v3 on v2

--- a/solution.py
+++ b/solution.py
@@ -15,9 +15,9 @@
 LOW, HIGH = 2 * SECTIONS, SECTIONS
 UNROLL = 8
 VMEM_BYTES = 60 << 20
-ROUND = 4
+ROUND = 8
 CHUNKS = 4
-PIECES = 4
+PIECES = 8
 GROUP = 8
 
 
@@ -146,8 +146,6 @@
                 start = blk * (species_here * 2 * rows) + g * (GROUP * 2 * rows) + l * rows + row
                 first[g, row + LOW, l, blk] = flat[pl.ds(start, GROUP, stride=2 * rows), :]
 
-    pl.semaphore_wait(door, groups - 1 + jnp.where(has_low, 1, 0) + jnp.where(has_high, 1, 0))
-
     def halo_up(g):
         return pltpu.make_async_remote_copy(
             src_ref=first.at[g, pl.ds(rows, LOW)],
@@ -188,30 +186,33 @@
             device_id_type=MESH,
         )
 
-    @pl.when(has_high)
-    def _():
-        coef_up().start()
-
-    @pl.when(has_low)
-    def _():
-        coef_down().start()
-
-    def send_edges(g, carry):
+    def turn_edges(g, carry):
         load(g, 0).wait()
         load(g, 1).wait()
-        for row in range(rows - LOW, rows):
+        for row in (*range(HIGH), *range(rows - LOW, rows)):
             turn(g, row)
+        return carry
+
+    lax.fori_loop(0, n_groups, turn_edges, 0)
+
+    pl.semaphore_wait(door, groups - 1 + jnp.where(has_low, 1, 0) + jnp.where(has_high, 1, 0))
+
+    @pl.when(has_high)
+    def _():
+        coef_up().start()
+
+    @pl.when(has_low)
+    def _():
+        coef_down().start()
+
+    def send_edges(g, carry):
+        @pl.when(has_low)
+        def _():
+            halo_down(g).start()
 
         @pl.when(has_high)
         def _():
             halo_up(g).start()
-
-        for row in range(HIGH):
-            turn(g, row)
-
-        @pl.when(has_low)
-        def _():
-            halo_down(g).start()
 
         return carry
 
@@ -543,22 +544,22 @@
             lax.fori_loop(0, 128 // ROUND, react, 0)
 
         def update(i, carry):
-            for j in range(8):
-                o = at8(i * 64 + j * 8)
+            for j in range(32):
+                o = at8(i * 256 + j * 8)
                 gain = made[0][o, :] + made[1][o, :]
                 loss = (lost_a[0][o, :] + lost_a[1][o, :]) + (lost_b[0][o, :] + lost_b[1][o, :])
                 target[o, :] = (source[o, :] + h * gain) / (1.0 + h * loss)
             return carry
 
         def update_piece(i, carry):
-            lax.fori_loop(i * (piece // 8), (i + 1) * (piece // 8), update, 0)
+            lax.fori_loop(i * (piece // 32), (i + 1) * (piece // 32), update, 0)
             out_piece(i).start()
             return carry
 
         if last:
             lax.fori_loop(0, PIECES, update_piece, 0)
         else:
-            lax.fori_loop(0, species // 8, update, 0)
+            lax.fori_loop(0, species // 32, update, 0)
     for i in range(PIECES):
         out_piece(i).wait()
 

time: 36.6 us -> 35.8 us (0.978)
  Pallas kernels: 36.2 us -> 35.4 us
    pallas_call x1, Pallas kernels: 9.05 us -> 8.31 us  [body(): pl.pallas_call(functools.partial(chemistry_kernel, reactions // 128), out...]
where the time goes in v3:
time: 35.8 us; the launch traced here: 35.4 us
  Pallas kernels  35.4 us (99%)
    pallas_call x1, Pallas kernels, body(): pl.pallas_call(functools.partial(transport_kernel, strips, groups), out_s...  27.1 us
    pallas_call x1, Pallas kernels, body(): pl.pallas_call(functools.partial(chemistry_kernel, reactions // 128), out...  8.31 us

profile of v3, /device:TPU:64, one launch (start us, length us, event | category | flops | bytes accessed | tf_op | source)
XLA Modules:
  0.0 35.4 jit_solution(16645056928853357222)
XLA Ops:
  0.0 27.1 %transport.1 = (f32[256,8,128]{2,1,0:T(8,128)}, f32[768,8,128]{2,1,0:T(8,128)}, s32[24,128]{1,0:T(8,128)}, f32[8,128]{1,0:T(8,128)}) custom-call(f32[32,2,16,256]{3,2,1,0:T(8,128)} %field.1, f32[2,16,256]{2,1,0:T(8,128)} %ux.1, f32[2,16,256]{2,1,0:T(8,128)} %uy.1, f32[2,16,256]{2,1,0:T(8,128)} %uz.1, f32[8,128]{1,0:T(8,128)} %bitcast.21, f32[8,128]{1,0:T(8,128)} %bitcast.22, ...), custom_call_target="tpu_custom_call" | custom-call | tf_op jit(solution)/shard_map/transport/pallas_call | solution.py:593
  27.1 8.3 %chemistry.1 = f32[2048,128]{1,0:T(8,128)} custom-call(s32[3072]{0:T(1024)} %bitcast.20, f32[2048,128]{1,0:T(8,128)} %bitcast.19, f32[6144,128]{1,0:T(8,128)} %bitcast.18, f32[8,128]{1,0:T(8,128)} %get-tuple-element.12.lit_in), custom_call_target="tpu_custom_call" | custom-call | tf_op jit(solution)/shard_map/chemistry/pallas_call | solution.py:650

commit v4 on v3

--- a/solution.py
+++ b/solution.py
@@ -16,7 +16,7 @@
 UNROLL = 8
 VMEM_BYTES = 60 << 20
 ROUND = 8
-CHUNKS = 4
+CHUNKS = 2
 PIECES = 8
 GROUP = 8
 
@@ -205,18 +205,23 @@
     def _():
         coef_down().start()
 
-    def send_edges(g, carry):
+    def send_up(g, carry):
+        @pl.when(has_high)
+        def _():
+            halo_up(g).start()
+
+        return carry
+
+    lax.fori_loop(0, n_groups, send_up, 0)
+
+    def send_down(g, carry):
         @pl.when(has_low)
         def _():
             halo_down(g).start()
 
-        @pl.when(has_high)
-        def _():
-            halo_up(g).start()
-
-        return carry
-
-    lax.fori_loop(0, n_groups, send_edges, 0)
+        return carry
+
+    lax.fori_loop(0, n_groups, send_down, 0)
 
     def turn_rest(g, carry):
         for row in range(HIGH, rows - LOW):
@@ -366,10 +371,6 @@
         def _():
             halo_up(g).wait_send()
 
-        @pl.when(has_low)
-        def _():
-            halo_down(g).wait_send()
-
         return carry
 
     def sweep_group(g, carry):
@@ -447,6 +448,10 @@
         coef_down().wait_send()
 
     def finish(g, carry):
+        @pl.when(has_low)
+        def _():
+            halo_down(g).wait_send()
+
         own_copy(g).wait()
         for i in order:
             all_copy(g, i).wait_send()

time: 35.8 us -> 35.6 us (level)
  no operation moved by 1% of the time
where the time goes in v4:
time: 35.6 us; the launch traced here: 35.3 us
  Pallas kernels  35.2 us (99%)
    pallas_call x1, Pallas kernels, body(): pl.pallas_call(functools.partial(transport_kernel, strips, groups), out_s...  27.1 us
    pallas_call x1, Pallas kernels, body(): pl.pallas_call(functools.partial(chemistry_kernel, reactions // 128), out...  8.12 us

profile of v4, /device:TPU:64, one launch (start us, length us, event | category | flops | bytes accessed | tf_op | source)
XLA Modules:
  0.0 35.3 jit_solution(2630853408511715199)
XLA Ops:
  0.0 27.1 %transport.1 = (f32[256,8,128]{2,1,0:T(8,128)}, f32[768,8,128]{2,1,0:T(8,128)}, s32[24,128]{1,0:T(8,128)}, f32[8,128]{1,0:T(8,128)}) custom-call(f32[32,2,16,256]{3,2,1,0:T(8,128)} %field.1, f32[2,16,256]{2,1,0:T(8,128)} %ux.1, f32[2,16,256]{2,1,0:T(8,128)} %uy.1, f32[2,16,256]{2,1,0:T(8,128)} %uz.1, f32[8,128]{1,0:T(8,128)} %bitcast.21, f32[8,128]{1,0:T(8,128)} %bitcast.22, ...), custom_call_target="tpu_custom_call" | custom-call | tf_op jit(solution)/shard_map/transport/pallas_call | solution.py:598
  27.1 8.1 %chemistry.1 = f32[2048,128]{1,0:T(8,128)} custom-call(s32[3072]{0:T(1024)} %bitcast.20, f32[2048,128]{1,0:T(8,128)} %bitcast.19, f32[6144,128]{1,0:T(8,128)} %bitcast.18, f32[8,128]{1,0:T(8,128)} %get-tuple-element.12.lit_in), custom_call_target="tpu_custom_call" | custom-call | tf_op jit(solution)/shard_map/chemistry/pallas_call | solution.py:655

commit v5 on v4

--- a/solution.py
+++ b/solution.py
@@ -138,12 +138,13 @@
                 edge_up[q, blk, l * 4 : l * 4 + 4] = plain[q, blk, l, rows - 4 : rows]
                 edge_down[q, blk, l * 4 : l * 4 + 4] = plain[q, blk, l, 0:4]
 
-    flat = raw.reshape(2 * species_here * 2 * rows, 128)
+    block_rows = (species_here + GROUP) * 2 * rows
+    flat = raw.reshape(2 * block_rows, 128)
 
     def turn(g, row):
         for l in range(2):
             for blk in range(2):
-                start = blk * (species_here * 2 * rows) + g * (GROUP * 2 * rows) + l * rows + row
+                start = blk * block_rows + g * (GROUP * 2 * rows) + l * rows + row
                 first[g, row + LOW, l, blk] = flat[pl.ds(start, GROUP, stride=2 * rows), :]
 
     def halo_up(g):
@@ -363,7 +364,7 @@
             own_sem.at[g],
         )
 
-    packed_flat = packed.reshape(n_groups * groups * GROUP * 8, 128)
+    packed_flat = packed.reshape((n_groups + 1) * groups * GROUP * 8, 128)
     order = [i for i in range(1, groups) if i % 2 == 1] + [i for i in range(1, groups) if i % 2 == 0]
 
     def halos_gone(g, carry):
@@ -606,11 +607,11 @@
         in_specs=[hbm] * 11,
         out_specs=(hbm, hbm, hbm, vmem),
         scratch_shapes=[
-            pltpu.VMEM((2, species_here, 2, rows, 128), F32),
+            pltpu.VMEM((2, species_here + GROUP, 2, rows, 128), F32),
             pltpu.VMEM((n_groups, rows + LOW + HIGH, 2, 2, GROUP, 128), F32),
             pltpu.VMEM((rows + 6, 2, 2, GROUP, 128), F32),
             pltpu.VMEM((rows + 3, 2, 2, GROUP, 128), F32),
-            pltpu.VMEM((n_groups, groups, GROUP, 8, 128), F32),
+            pltpu.VMEM((n_groups + 1, groups, GROUP, 8, 128), F32),
             pltpu.VMEM((6, rows + 7, 2, 2, GROUP, 128), F32),
             pltpu.VMEM((3, 2, 2, rows, 128), F32),
             pltpu.VMEM((3, 2, 8, 128), F32),

time: 35.6 us -> 35.6 us (level)
  no operation moved by 1% of the time
where the time goes in v5:
time: 35.6 us; the launch traced here: 35.3 us
  Pallas kernels  35.3 us (99%)
    pallas_call x1, Pallas kernels, body(): pl.pallas_call(functools.partial(transport_kernel, strips, groups), out_s...  27.1 us
    pallas_call x1, Pallas kernels, body(): pl.pallas_call(functools.partial(chemistry_kernel, reactions // 128), out...  8.13 us

profile of v5, /device:TPU:64, one launch (start us, length us, event | category | flops | bytes accessed | tf_op | source)
XLA Modules:
  0.0 35.3 jit_solution(5715921895008185021)
XLA Ops:
  0.0 27.1 %transport.1 = (f32[256,8,128]{2,1,0:T(8,128)}, f32[768,8,128]{2,1,0:T(8,128)}, s32[24,128]{1,0:T(8,128)}, f32[8,128]{1,0:T(8,128)}) custom-call(f32[32,2,16,256]{3,2,1,0:T(8,128)} %field.1, f32[2,16,256]{2,1,0:T(8,128)} %ux.1, f32[2,16,256]{2,1,0:T(8,128)} %uy.1, f32[2,16,256]{2,1,0:T(8,128)} %uz.1, f32[8,128]{1,0:T(8,128)} %bitcast.21, f32[8,128]{1,0:T(8,128)} %bitcast.22, ...), custom_call_target="tpu_custom_call" | custom-call | tf_op jit(solution)/shard_map/transport/pallas_call | solution.py:599
  27.1 8.1 %chemistry.1 = f32[2048,128]{1,0:T(8,128)} custom-call(s32[3072]{0:T(1024)} %bitcast.20, f32[2048,128]{1,0:T(8,128)} %bitcast.19, f32[6144,128]{1,0:T(8,128)} %bitcast.18, f32[8,128]{1,0:T(8,128)} %get-tuple-element.12.lit_in), custom_call_target="tpu_custom_call" | custom-call | tf_op jit(solution)/shard_map/chemistry/pallas_call | solution.py:656

commit v6 on v5

--- a/solution.py
+++ b/solution.py
@@ -475,7 +475,7 @@
 def chemistry_kernel(ways, table_in, cells_in, rates_in, lit_in, out, *scratch):
     cells, rates, lit, result, middle = scratch[:5]
     sums = scratch[5 : 5 + 6 * DAY_STEPS]
-    table = scratch[5 + 6 * DAY_STEPS : 5 + 6 * DAY_STEPS + 3 * ways]
+    table = scratch[5 + 6 * DAY_STEPS : 5 + 6 * DAY_STEPS + 3 * ways // 2]
     first_sem, table_sem, rate_sem, out_sem = scratch[-4:]
     species = cells.shape[0] // 8
     zero = jnp.zeros((8, 128), F32)
@@ -484,8 +484,8 @@
         pltpu.make_async_copy(source, target, first_sem.at[i])
         for i, (source, target) in enumerate(((cells_in, cells), (lit_in, lit)))
     ] + [
-        pltpu.make_async_copy(table_in.at[pl.ds(n * 128, 128)], table[n], table_sem.at[n])
-        for n in range(3 * ways)
+        pltpu.make_async_copy(table_in.at[pl.ds(n * 256, 256)], table[n], table_sem.at[n])
+        for n in range(3 * ways // 2)
     ]
     part = 128 // CHUNKS
 
@@ -528,7 +528,7 @@
                 for w in range(0, ways, 2):
                     new = []
                     for k in range(2):
-                        a, b, p = (at8(table[q * ways + w + k][i]) for q in range(3))
+                        a, b, p = (at8(table[(q * ways + w) // 2][k * 128 + i]) for q in range(3))
                         rate = rates[at8(n * (ROUND * ways * 8) + (j * ways + w + k) * 8), :]
                         ca, cb = source[a, :], source[b, :]
                         by_a = rate * cb
@@ -664,8 +664,8 @@
             pltpu.VMEM((8, 128), F32),
         ]
         + [pltpu.VMEM((species * 8, 128), F32)] * (2 + 6 * DAY_STEPS)
-        + [pltpu.SMEM((128,), jnp.int32)] * (3 * (reactions // 128))
-        + [dma((2,)), dma((3 * (reactions // 128),)), dma((CHUNKS,)), dma((PIECES,))],
+        + [pltpu.SMEM((256,), jnp.int32)] * (3 * (reactions // 256))
+        + [dma((2,)), dma((3 * (reactions // 256),)), dma((CHUNKS,)), dma((PIECES,))],
         compiler_params=pltpu.CompilerParams(vmem_limit_bytes=VMEM_BYTES),
         name="chemistry",
     )(

time: 35.6 us -> 35.5 us (level)
  no operation moved by 1% of the time
where the time goes in v6:
time: 35.5 us; the launch traced here: 35.2 us
  Pallas kernels  35.2 us (99%)
    pallas_call x1, Pallas kernels, body(): pl.pallas_call(functools.partial(transport_kernel, strips, groups), out_s...  27.1 us
    pallas_call x1, Pallas kernels, body(): pl.pallas_call(functools.partial(chemistry_kernel, reactions // 128), out...  8.05 us

profile of v6, /device:TPU:64, one launch (start us, length us, event | category | flops | bytes accessed | tf_op | source)
XLA Modules:
  0.0 35.2 jit_solution(13451207674309180324)
XLA Ops:
  0.0 27.1 %transport.1 = (f32[256,8,128]{2,1,0:T(8,128)}, f32[768,8,128]{2,1,0:T(8,128)}, s32[24,128]{1,0:T(8,128)}, f32[8,128]{1,0:T(8,128)}) custom-call(f32[32,2,16,256]{3,2,1,0:T(8,128)} %field.1, f32[2,16,256]{2,1,0:T(8,128)} %ux.1, f32[2,16,256]{2,1,0:T(8,128)} %uy.1, f32[2,16,256]{2,1,0:T(8,128)} %uz.1, f32[8,128]{1,0:T(8,128)} %bitcast.21, f32[8,128]{1,0:T(8,128)} %bitcast.22, ...), custom_call_target="tpu_custom_call" | custom-call | tf_op jit(solution)/shard_map/transport/pallas_call | solution.py:599
  27.1 8.1 %chemistry.1 = f32[2048,128]{1,0:T(8,128)} custom-call(s32[3072]{0:T(1024)} %bitcast.20, f32[2048,128]{1,0:T(8,128)} %bitcast.19, f32[6144,128]{1,0:T(8,128)} %bitcast.18, f32[8,128]{1,0:T(8,128)} %get-tuple-element.12.lit_in), custom_call_target="tpu_custom_call" | custom-call | tf_op jit(solution)/shard_map/chemistry/pallas_call | solution.py:656
